TPU v7x, 32 devices: a whole 2x2x4 slice. The times are simulated.
32 devices in a mesh: grp: 2 (over y), seq: 16 (over z, x, core).
Axes of the slice: x: 2, y: 2, z: 4, core: 2. Of those that a mesh axis runs over, the one named last changes fastest.
Arguments:
- queries: bfloat16 [4096, 128], P(('grp', 'seq')), parts along dimension 0, may hold values from -6 to 6
- keys: bfloat16 [4096, 128], P(('grp', 'seq')), parts along dimension 0, may hold values from -6 to 6
- values: bfloat16 [4096, 128], P(('grp', 'seq')), parts along dimension 0, may hold values from -6 to 6
- log_gate: float32 [4096], P(('grp', 'seq')), parts along dimension 0, may hold values from -1 to 0, as said below
- out_grad: bfloat16 [4096, 128], P(('grp', 'seq')), parts along dimension 0, may hold values from -6 to 6
- segment_order: int32 [64], P(('grp', 'seq')), parts along dimension 0, may hold values from 0 to 31, each once
Outputs:
- attn_out: bfloat16 [4096, 128], P(('grp', 'seq')), parts along dimension 0
- query_grad: float32 [4096, 128], P(('grp', 'seq')), parts along dimension 0
- key_grad: float32 [4096, 128], P(('grp', 'seq')), parts along dimension 0
- value_grad: float32 [4096, 128], P(('grp', 'seq')), parts along dimension 0
- gate_grad: float32 [4096], P(('grp', 'seq')), parts along dimension 0
There are 2 independent parts, one for each index of `grp`. A program takes and returns all parts, laid end to end along the dimension named above; each array names one. Nothing has to cross between parts.
Inputs may be any that keep to these rules, and one draw needn't show every extreme that they name: `log_gate`: every gate is below one. `segment_order`: each segment index appears once.
All inputs are finite; a program needn't handle non-finite values.
Results may differ from a plain program's by a relative error of at most 0.0095.
Values may be sent and summed in bfloat16 or wider, within the bound.
A program may use at most 64 MiB of HBM per device.

v0:
```python
import jax
import jax.numpy as jnp
from jax import lax
from jax.sharding import PartitionSpec as P

masked_value = -1e30


def contract_last(left, right):
    return lax.dot_general(
        left, right, (((1,), (1,)), ((), ())), preferred_element_type=jnp.float32
    )


def contract_first(left, right):
    return lax.dot_general(
        left, right, (((0,), (0,)), ((), ())), preferred_element_type=jnp.float32
    )


def tile_scores(query_rows, query_gate, query_pos, key_rows, key_gate, key_pos, score_scale):
    scores = (
        contract_last(query_rows, key_rows) * score_scale + query_gate[:, None] - key_gate[None, :]
    )
    visible = key_pos[None, :] <= query_pos[:, None]
    return (scores, visible)


def tile_probs(scores, visible, row_total):
    return jnp.where(visible, jnp.exp(scores - row_total[:, None]), 0.0)


def local(queries, keys, values, log_gate, out_grad, segment_order):
    tokens_here, width = queries.shape
    devices = lax.axis_size("seq")
    segment_rows = tokens_here // 2
    total_len = tokens_here * devices
    score_scale = width ** (-0.5)
    offsets_in = lax.broadcasted_iota(jnp.int32, (1, segment_rows), 1)
    local_cum = jnp.cumsum(log_gate.reshape(2, segment_rows), axis=1)
    segment_total = local_cum[:, -1]
    segment_place = segment_order.astype(jnp.float32)
    own_pos = (segment_order[:, None] * segment_rows + offsets_in).reshape(-1)
    all_totals, all_place = (
        lax.all_gather(segment_total, "seq", axis=0, tiled=True),
        lax.all_gather(segment_place, "seq", axis=0, tiled=True),
    )
    earlier = (all_place[None, :] < segment_place[:, None]).astype(jnp.float32)
    own_offset = jnp.sum(earlier * all_totals[None, :], axis=1)
    own_gate = (local_cum + own_offset[:, None]).reshape(-1)
    all_gate = lax.all_gather(own_gate, "seq", axis=0, tiled=True)
    all_pos = (all_place.astype(jnp.int32)[:, None] * segment_rows + offsets_in).reshape(-1)
    key_all, value_all = (
        lax.all_gather(keys, "seq", axis=0, tiled=True),
        lax.all_gather(values, "seq", axis=0, tiled=True),
    )
    block = 2048
    count = total_len // block

    def key_tile(block_index):
        start = block_index * block
        return (
            lax.dynamic_slice_in_dim(key_all, start, block),
            lax.dynamic_slice_in_dim(value_all, start, block),
            lax.dynamic_slice_in_dim(all_gate, start, block),
            lax.dynamic_slice_in_dim(all_pos, start, block),
        )

    def stats_step(block_index, carry):
        run_max, run_sum = carry
        key_rows, value_rows, key_gate, key_pos = key_tile(block_index)
        scores, visible = tile_scores(
            queries, own_gate, own_pos, key_rows, key_gate, key_pos, score_scale
        )
        kept = jnp.where(visible, scores, masked_value)
        new_max = jnp.maximum(run_max, jnp.max(kept, axis=1))
        fresh = jnp.sum(jnp.where(visible, jnp.exp(kept - new_max[:, None]), 0.0), axis=1)
        return (new_max, run_sum * jnp.exp(run_max - new_max) + fresh)

    start_max = jnp.full((tokens_here,), masked_value, jnp.float32)
    run_max, run_sum = lax.fori_loop(
        0, count, stats_step, (start_max, jnp.zeros((tokens_here,), jnp.float32))
    )
    log_total = run_max + jnp.log(run_sum)

    def output_step(block_index, total):
        key_rows, value_rows, key_gate, key_pos = key_tile(block_index)
        scores, visible = tile_scores(
            queries, own_gate, own_pos, key_rows, key_gate, key_pos, score_scale
        )
        probs = tile_probs(scores, visible, log_total).astype(jnp.bfloat16)
        return total + jnp.dot(probs, value_rows, preferred_element_type=jnp.float32)

    out_full = lax.fori_loop(0, count, output_step, jnp.zeros((tokens_here, width), jnp.float32))
    attn_out = out_full.astype(jnp.bfloat16)
    row_delta = jnp.sum(out_grad.astype(jnp.float32) * out_full, axis=1)

    def row_terms(block_index):
        key_rows, value_rows, key_gate, key_pos = key_tile(block_index)
        scores, visible = tile_scores(
            queries, own_gate, own_pos, key_rows, key_gate, key_pos, score_scale
        )
        probs = tile_probs(scores, visible, log_total)
        dprob = contract_last(out_grad, value_rows)
        return (key_rows, probs, probs * (dprob - row_delta[:, None]))

    def query_step(block_index, total):
        key_rows, probs, dscore = row_terms(block_index)
        return total + jnp.dot(
            dscore.astype(jnp.bfloat16), key_rows, preferred_element_type=jnp.float32
        )

    query_acc = lax.fori_loop(0, count, query_step, jnp.zeros((tokens_here, width), jnp.float32))
    query_all, grad_all = (
        lax.all_gather(queries, "seq", axis=0, tiled=True),
        lax.all_gather(out_grad, "seq", axis=0, tiled=True),
    )
    total_all, delta_all = (
        lax.all_gather(log_total, "seq", axis=0, tiled=True),
        lax.all_gather(row_delta, "seq", axis=0, tiled=True),
    )

    def column_step(block_index, carry):
        key_acc, value_acc, column_acc = carry
        start = block_index * block
        query_rows = lax.dynamic_slice_in_dim(query_all, start, block)
        grad_rows = lax.dynamic_slice_in_dim(grad_all, start, block)
        scores, visible = tile_scores(
            query_rows,
            lax.dynamic_slice_in_dim(all_gate, start, block),
            lax.dynamic_slice_in_dim(all_pos, start, block),
            keys,
            own_gate,
            own_pos,
            score_scale,
        )
        probs = tile_probs(scores, visible, lax.dynamic_slice_in_dim(total_all, start, block))
        dprob = contract_last(grad_rows, values)
        dscore = probs * (dprob - lax.dynamic_slice_in_dim(delta_all, start, block)[:, None])
        dscore_low = dscore.astype(jnp.bfloat16)
        key_acc = key_acc + contract_first(dscore_low, query_rows) * score_scale
        value_acc = value_acc + contract_first(probs.astype(jnp.bfloat16), grad_rows)
        column_acc = column_acc - jnp.sum(dscore, axis=0)
        return (key_acc, value_acc, column_acc)

    zeros_own = jnp.zeros((tokens_here, width), jnp.float32)
    key_grad, value_grad, gate_point = lax.fori_loop(
        0, count, column_step, (zeros_own, zeros_own, jnp.zeros((tokens_here,), jnp.float32))
    )
    query_grad = query_acc * score_scale
    point_rows = gate_point.reshape(2, segment_rows)
    within = jnp.flip(jnp.cumsum(jnp.flip(point_rows, 1), axis=1), 1)
    all_point = lax.all_gather(within[:, 0], "seq", axis=0, tiled=True)
    later = (all_place[None, :] > segment_place[:, None]).astype(jnp.float32)
    gate_grad = (within + jnp.sum(later * all_point[None, :], axis=1)[:, None]).reshape(-1)
    return (attn_out, query_grad, key_grad, value_grad, gate_grad)


def solution(mesh):
    placed = (
        P(("grp", "seq"), None),
        P(("grp", "seq"), None),
        P(("grp", "seq"), None),
        P(("grp", "seq")),
        P(("grp", "seq"), None),
        P(("grp", "seq")),
    )
    return jax.shard_map(
        local,
        mesh=mesh,
        in_specs=placed,
        out_specs=(
            P(("grp", "seq"), None),
            P(("grp", "seq"), None),
            P(("grp", "seq"), None),
            P(("grp", "seq"), None),
            P(("grp", "seq")),
        ),
        check_vma=False,
    )
```

profile of v0, /device:TPU:0, one launch (start us, length us, event | category | flops | bytes accessed | tf_op | source)
XLA Modules:
  0.0 211.2 jit_solution(15644140626693972713)
XLA Ops:
  0.6 0.9 copy.17
  1.5 24.6 %all_gather.34 = bf16[2048,128]{1,0:T(8,128)(2,1)S(1)} all-gather(bf16[128,128]{1,0:T(8,128)(2,1)S(1)} %copy-done), channel_id=1, replica_groups=mesh['grp'=2,'seq'=16] {'seq'}, dimensions={0}, use_global_device_ids=true | all-gather | bytes 557056 | tf_op jit(solution)/shard_map/all_gather | solution.py:55
  26.2 0.2 reduce_window_sum.17
  26.4 0.2 slice_reduce_fusion.1
  26.6 0.6 copy-done.6
  27.3 0.6 dynamic-slice
  28.5 0.2 dynamic-update-slice.1
  28.8 0.7 copy-done.5
  29.5 29.8 %all-reduce.3 = (f32[32]{0:T(128)S(1)}, f32[32]{0:T(128)S(1)}) all-reduce(f32[32]{0:T(128)S(1)} %dynamic-update-slice.1, f32[32]{0:T(128)S(1)} %convert_dynamic-update-slice_fusion), channel_id=2, replica_groups=mesh['grp'=2,'seq'=16] {'seq'}, use_global_device_ids=true, to_apply=%add.1 | all-reduce | flops 64 | bytes 512
  59.7 0.2 fusion.29
  60.0 17.0 %all-gather.2 = f32[16,1,128]{2,1,0:T(1,128)S(1)} all-gather(f32[1,1,128]{2,1,0:T(1,128)S(1)} %reshape.142), channel_id=1, replica_groups=mesh['grp'=2,'seq'=16] {'seq'}, dimensions={0}, use_global_device_ids=true | all-gather | bytes 8704 | tf_op jit(solution)/shard_map/all_gather | solution.py:51
  77.1 20.7 %all_gather.31 = bf16[2048,128]{1,0:T(8,128)(2,1)S(1)} all-gather(bf16[128,128]{1,0:T(8,128)(2,1)S(1)} %copy-done.3), channel_id=1, replica_groups=mesh['grp'=2,'seq'=16] {'seq'}, dimensions={0}, use_global_device_ids=true | all-gather | bytes 557056 | tf_op jit(solution)/shard_map/all_gather | solution.py:54
  97.8 0.5 fusion.13
  98.3 0.4 fusion.12
  98.7 0.5 multiply_reduce_fusion
  99.2 0.7 copy.18
  99.9 1.2 fusion.11
  101.1 18.9 %all_gather.35 = bf16[2048,128]{1,0:T(8,128)(2,1)S(1)} all-gather(bf16[128,128]{1,0:T(8,128)(2,1)S(1)} %copy-done.2), channel_id=1, replica_groups=mesh['grp'=2,'seq'=16] {'seq'}, dimensions={0}, use_global_device_ids=true | all-gather | bytes 557056 | tf_op jit(solution)/shard_map/all_gather | solution.py:115
  120.0 18.7 %all-gather.3 = f32[16,1,128]{2,1,0:T(1,128)S(1)} all-gather(f32[1,1,128]{2,1,0:T(1,128)S(1)} %bitcast.24), channel_id=1, replica_groups=mesh['grp'=2,'seq'=16] {'seq'}, dimensions={0}, use_global_device_ids=true | all-gather | bytes 8704 | tf_op jit(solution)/shard_map/all_gather | solution.py:119
  138.6 0.9 fusion.5
  139.5 17.3 %all-gather.4 = f32[16,1,128]{2,1,0:T(1,128)S(1)} all-gather(f32[1,1,128]{2,1,0:T(1,128)S(1)} %bitcast.23), channel_id=1, replica_groups=mesh['grp'=2,'seq'=16] {'seq'}, dimensions={0}, use_global_device_ids=true | all-gather | bytes 8704 | tf_op jit(solution)/shard_map/all_gather | solution.py:120
  156.9 20.3 %all_gather.37 = bf16[2048,128]{1,0:T(8,128)(2,1)S(1)} all-gather(bf16[128,128]{1,0:T(8,128)(2,1)S(1)} %copy-done.1), channel_id=1, replica_groups=mesh['grp'=2,'seq'=16] {'seq'}, dimensions={0}, use_global_device_ids=true | all-gather | bytes 557056 | tf_op jit(solution)/shard_map/all_gather | solution.py:116
  177.2 0.4 fusion.33
  177.6 1.0 convolution_multiply_fusion.2
  178.6 1.0 fusion.17
  179.6 0.1 reverse.4
  179.7 0.2 reduce_window_sum.18
  180.1 0.2 slice_reduce_fusion
  180.3 0.2 dynamic-update-slice.2
  180.5 29.8 %all-reduce.2 = f32[32]{0:T(128)S(1)} all-reduce(f32[32]{0:T(128)S(1)} %dynamic-update-slice.2), channel_id=3, replica_groups=mesh['grp'=2,'seq'=16] {'seq'}, use_global_device_ids=true, to_apply=%add.2 | all-reduce | flops 32 | bytes 256
  210.3 0.2 fusion.30
  210.6 0.6 reshape.130
  (32 shorter events, 1.1 us)
Async XLA Ops:
  0.6 0.9 copy-start
  1.5 24.6 %copy-start.4 = (f32[128]{0:T(128)S(1)}, f32[128]{0:T(128)}, u32[]{:S(2)}) copy-start(f32[128]{0:T(128)} %param.9) | copy-start | bytes 1540
  26.6 0.7 copy-start.6
  28.8 0.7 copy-start.5
  59.3 17.8 %copy-start.3 = (bf16[128,128]{1,0:T(8,128)(2,1)S(1)}, bf16[128,128]{1,0:T(8,128)(2,1)}, u32[]{:S(2)}) copy-start(bf16[128,128]{1,0:T(8,128)(2,1)} %param.7) | copy-start | bytes 98308
  77.1 20.7 %copy-start.2 = (bf16[128,128]{1,0:T(8,128)(2,1)S(1)}, bf16[128,128]{1,0:T(8,128)(2,1)}, u32[]{:S(2)}) copy-start(bf16[128,128]{1,0:T(8,128)(2,1)} %param.6) | copy-start | bytes 98308
  99.2 0.8 copy-start.1
where the time goes:
time: 212 us; the launch traced here: 211 us
  blocking collectives  197 us (93%)
  local copies, waits for them, and re-layouts  5.65 us (3%)
  matrix products  5.38 us (3%)
    unnamed x2, blocking collectives  59.6 us
    all_gather x1, blocking collectives, local(): lax.all_gather(values, 'seq', axis=0, tiled=True)  24.6 us
    all_gather x1, blocking collectives, local(): lax.all_gather(keys, 'seq', axis=0, tiled=True)  20.7 us
    all_gather x1, blocking collectives, local(): lax.all_gather(out_grad, 'seq', axis=0, tiled=True)  20.3 us
    all_gather x1, blocking collectives, local(): lax.all_gather(queries, 'seq', axis=0, tiled=True)  18.9 us
    all_gather x1, blocking collectives, local(): lax.all_gather(log_total, 'seq', axis=0, tiled=True)  18.7 us
    all_gather x1, blocking collectives, local(): lax.all_gather(row_delta, 'seq', axis=0, tiled=True)  17.3 us
    all_gather x1, blocking collectives, local(): all_gate = lax.all_gather(own_gate, 'seq', axis=0, tiled=True)  17 us

commit v1 on v0

v1 whole, which is shorter than its diff:
```python
import functools
import math

import jax
import jax.numpy as jnp
from jax import lax
from jax.experimental import pallas as pl
from jax.experimental.pallas import tpu as pltpu
from jax.sharding import PartitionSpec as P

MESH = pl.DeviceIdType.MESH
HIDDEN = -1e30
FLOOR = -1e29
LOG2E = math.log2(math.e)


def dot(left, right, left_dim, right_dim):
    return lax.dot_general(
        left, right, (((left_dim,), (right_dim,)), ((), ())), preferred_element_type=jnp.float32
    )


def for_each(count, body):
    if count <= 4:
        for index in range(count):
            body(index)
    else:
        lax.fori_loop(0, count, lambda index, carry: (body(index), carry)[1], 0)


def kernel(
    rows,
    cols,
    halves,
    q_hbm,
    k_hbm,
    v_hbm,
    gate_hbm,
    g_hbm,
    order_ref,
    out_ref,
    dq_ref,
    dk_ref,
    dv_ref,
    dgate_ref,
    gate_ref,
    load_sems,
    meta,
    pts_out,
    pts_in,
    cum,
    place,
    q_all,
    g_all,
    k_all,
    v_all,
    p_all,
    dp_all,
    part_stat,
    stats,
    deltas,
    p_low,
    ds_low,
    dk_out,
    dv_out,
    dk_in,
    dv_in,
    o_out,
    dq_out,
    o_in,
    dq_in,
    meta_send,
    meta_recv,
    pts_send,
    pts_recv,
    q_send,
    q_recv,
    k_send,
    k_recv,
    stat_send,
    stat_recv,
    delta_send,
    delta_recv,
    kout_send,
    kout_recv,
    qout_send,
    qout_recv,
):
    devices = rows * cols
    tokens, width = q_hbm.shape
    piece = tokens // halves
    queries = cols * tokens
    scale = width ** (-0.5)
    grp = lax.axis_index("grp")
    me = lax.axis_index("seq")
    my_row = me // cols
    my_col = me % cols

    def at(index):
        return (grp, index)

    def other(shift):
        return lax.rem(me + shift, devices)

    def in_row(shift):
        return my_row * cols + lax.rem(my_col + shift, cols)

    def in_column(shift):
        return lax.rem(my_row + shift, rows) * cols + my_col

    barrier = pltpu.get_barrier_semaphore()

    def greet(shift):
        pl.semaphore_signal(barrier, inc=1, device_id=at(other(shift + 1)), device_id_type=MESH)

    lax.fori_loop(0, devices - 1, lambda i, c: (greet(i), c)[1], 0)

    q_ref, g_ref, k_ref, v_ref = q_all.at[0], g_all.at[0], k_all.at[0], v_all.at[0]
    loads = [
        pltpu.make_async_copy(source, target, load_sems.at[index])
        for index, (source, target) in enumerate(
            (
                (gate_hbm, gate_ref),
                (q_hbm, q_ref),
                (k_hbm, k_ref),
                (g_hbm, g_ref),
                (v_hbm, v_ref),
            )
        )
    ]
    for load in loads:
        load.start()
    loads[0].wait()

    lane = lax.broadcasted_iota(jnp.int32, (tokens, tokens), 1)
    line = lax.broadcasted_iota(jnp.int32, (tokens, tokens), 0)
    same = lane // piece == line // piece
    diagonal = lane == line

    def to_column(row):
        return jnp.sum(jnp.where(diagonal, row, 0.0), axis=1, keepdims=True)

    def to_row(column):
        return jnp.sum(jnp.where(diagonal, column, 0.0), axis=0, keepdims=True)

    gate_row = gate_ref[...].reshape(1, tokens)
    local_cum = jnp.sum(
        jnp.where(same & (line <= lane), to_column(gate_row), 0.0), axis=0, keepdims=True
    )
    lane_row = lax.broadcasted_iota(jnp.int32, (1, tokens), 1)
    own_order = jnp.zeros((1, tokens), jnp.float32)
    for half in range(halves):
        own_order = jnp.where(
            lane_row // piece == half, order_ref[half].astype(jnp.float32), own_order
        )
    meta[pl.ds(me, 1), 0:1, :] = local_cum.reshape(1, 1, tokens)
    meta[pl.ds(me, 1), 1:2, :] = own_order.reshape(1, 1, tokens)
    for load in loads[1:]:
        load.wait()

    pl.semaphore_wait(barrier, devices - 1)

    def meta_copy(shift):
        return pltpu.make_async_remote_copy(
            src_ref=meta.at[me],
            dst_ref=meta.at[me],
            send_sem=meta_send.at[shift],
            recv_sem=meta_recv.at[shift],
            device_id=at(other(shift)),
            device_id_type=MESH,
        )

    def meta_arrival(shift):
        source = lax.rem(me + devices - shift, devices)
        return pltpu.make_async_remote_copy(
            src_ref=meta.at[source],
            dst_ref=meta.at[source],
            send_sem=meta_send.at[shift],
            recv_sem=meta_recv.at[shift],
            device_id=at(other(shift)),
            device_id_type=MESH,
        )

    def row_copy(which, shift):
        ref, slots = ((q_ref, q_all), (g_ref, g_all))[which]
        return pltpu.make_async_remote_copy(
            src_ref=ref,
            dst_ref=slots.at[cols - shift],
            send_sem=q_send.at[which, shift],
            recv_sem=q_recv.at[which, cols - shift],
            device_id=at(in_row(shift)),
            device_id_type=MESH,
        )

    def column_copy(which, shift):
        ref, slots = ((k_ref, k_all), (v_ref, v_all))[which]
        return pltpu.make_async_remote_copy(
            src_ref=ref,
            dst_ref=slots.at[rows - shift],
            send_sem=k_send.at[which, shift],
            recv_sem=k_recv.at[which, rows - shift],
            device_id=at(in_column(shift)),
            device_id_type=MESH,
        )

    lax.fori_loop(1, devices, lambda i, c: (meta_copy(i).start(), c)[1], 0)
    for which in range(2):
        for shift in range(1, cols):
            row_copy(which, shift).start()
        for shift in range(1, rows):
            column_copy(which, shift).start()

    lax.fori_loop(1, devices, lambda i, c: (meta_arrival(i).wait_recv(), c)[1], 0)

    orders = meta[:, 1, :]
    base = meta[:, 0, :]
    total = base
    for half in range(halves):
        totals = base[:, (half + 1) * piece - 1 : (half + 1) * piece]
        heads = orders[:, half * piece : half * piece + 1]

        for device in range(devices):
            earlier = heads[device : device + 1, :] < orders
            total = total + jnp.where(earlier, totals[device : device + 1, :], 0.0)
    cum[...] = total * LOG2E
    within = (lax.broadcasted_iota(jnp.int32, (devices, tokens), 1) % piece).astype(jnp.float32)
    place[...] = orders * piece + within

    query_cum = jnp.concatenate([cum[pl.ds(in_row(s), 1), :] for s in range(cols)], axis=1)
    query_place = jnp.concatenate([place[pl.ds(in_row(s), 1), :] for s in range(cols)], axis=1)

    for shift in range(1, cols):
        row_copy(0, cols - shift).wait_recv()

    def first_pass(slot):
        source = in_column(slot)
        key_cum = to_column(cum[pl.ds(source, 1), :])
        key_place = to_column(place[pl.ds(source, 1), :])
        if isinstance(slot, int) and slot == 0:
            pass
        else:
            arrived(0, slot)
        scores = dot(k_all[slot], q_all[...].reshape(queries, width), 1, 1)
        scores = scores * (scale * LOG2E) + (query_cum - key_cum)
        scores = jnp.where(key_place <= query_place, scores, HIDDEN)
        top = jnp.maximum(jnp.max(scores, axis=0, keepdims=True), FLOOR)
        probs = jnp.exp2(scores - top)
        p_all[slot] = probs
        part_stat[slot, 0:1, :] = top
        part_stat[slot, 1:2, :] = jnp.sum(probs, axis=0, keepdims=True)

    def arrived(which, slot):
        ref, slots = ((k_ref, k_all), (v_ref, v_all))[which]
        pltpu.make_async_remote_copy(
            src_ref=ref,
            dst_ref=slots.at[slot],
            send_sem=k_send.at[which, slot],
            recv_sem=k_recv.at[which, slot],
            device_id=at(in_column(slot)),
            device_id_type=MESH,
        ).wait_recv()

    first_pass(0)
    for_each(rows - 1, lambda i: first_pass(i + 1))

    tops = part_stat[:, 0, :]
    top = jnp.max(tops, axis=0, keepdims=True)
    shrink = jnp.exp2(tops - top)
    stats[0, 0:1, :] = top
    stats[0, 1:2, :] = jnp.sum(part_stat[:, 1, :] * shrink, axis=0, keepdims=True)

    def stat_copy(shift):
        return pltpu.make_async_remote_copy(
            src_ref=stats.at[0],
            dst_ref=stats.at[cols - shift],
            send_sem=stat_send.at[shift],
            recv_sem=stat_recv.at[cols - shift],
            device_id=at(in_row(shift)),
            device_id_type=MESH,
        )

    for shift in range(1, cols):
        stat_copy(shift).start()

    for shift in range(1, cols):
        row_copy(1, cols - shift).wait_recv()
    for shift in range(1, cols):
        stat_copy(cols - shift).wait_recv()

    def turn(turned, slot):
        cut = (cols - slot) * tokens
        return jnp.concatenate([turned[:, cut:], turned[:, :cut]], axis=1)

    aligned = [stats[0]] + [turn(stats[slot], slot) for slot in range(1, cols)]
    top = functools.reduce(jnp.maximum, [part[0:1, :] for part in aligned])
    sums = functools.reduce(
        jnp.add, [jnp.exp2(part[0:1, :] - top) * part[1:2, :] for part in aligned]
    )
    inverse = 1.0 / sums

    def normalise(slot):
        if not (isinstance(slot, int) and slot == 0):
            arrived(1, slot)
        dprobs = dot(v_all[slot], g_all[...].reshape(queries, width), 1, 1)
        probs = p_all[slot] * (jnp.exp2(part_stat[slot, 0:1, :] - top) * inverse)
        low = probs.astype(jnp.bfloat16)
        p_all[slot] = probs
        p_low[slot] = low
        dp_all[slot] = dprobs
        part_stat[slot, 2:3, :] = jnp.sum(
            low.astype(jnp.float32) * dprobs, axis=0, keepdims=True
        )

    normalise(0)
    for_each(rows - 1, lambda i: normalise(i + 1))
    deltas[0] = jnp.sum(part_stat[:, 2, :], axis=0, keepdims=True)

    def delta_copy(shift):
        return pltpu.make_async_remote_copy(
            src_ref=deltas.at[0],
            dst_ref=deltas.at[cols - shift],
            send_sem=delta_send.at[shift],
            recv_sem=delta_recv.at[cols - shift],
            device_id=at(in_row(shift)),
            device_id_type=MESH,
        )

    for shift in range(1, cols):
        delta_copy(shift).start()

    def column_out(which, slot):
        source, target = ((dk_out, dk_in), (dv_out, dv_in))[which]
        return pltpu.make_async_remote_copy(
            src_ref=source.at[slot],
            dst_ref=target.at[rows - slot],
            send_sem=kout_send.at[which, slot],
            recv_sem=kout_recv.at[which, rows - slot],
            device_id=at(in_column(slot)),
            device_id_type=MESH,
        )

    def value_pass(slot):
        value_part = dot(p_low[slot], g_all[...].reshape(queries, width), 1, 0)
        if isinstance(slot, int) and slot == 0:
            dv_ref[...] = value_part
        else:
            dv_out[slot] = value_part.astype(jnp.bfloat16)
            column_out(1, slot).start()

    for_each(rows - 1, lambda i: value_pass(i + 1))

    def row_out(which, slot):
        source, target = ((o_out, o_in), (dq_out, dq_in))[which]
        return pltpu.make_async_remote_copy(
            src_ref=source.at[slot],
            dst_ref=target.at[cols - slot],
            send_sem=qout_send.at[which, slot],
            recv_sem=qout_recv.at[which, cols - slot],
            device_id=at(in_row(slot)),
            device_id_type=MESH,
        )

    p_flat = p_low[...].reshape(rows * tokens, queries)
    v_flat = v_all[...].reshape(rows * tokens, width)
    out_part = dot(v_flat, p_flat, 0, 0)
    for slot in range(1, cols):
        o_out[slot] = out_part[:, slot * tokens : (slot + 1) * tokens].astype(jnp.bfloat16)
        row_out(0, slot).start()

    for shift in range(1, cols):
        delta_copy(cols - shift).wait_recv()
    delta = deltas[0]
    for slot in range(1, cols):
        delta = delta + turn(deltas[slot], slot)

    def second_pass(slot):
        dscore = p_all[slot] * (dp_all[slot] - delta)
        ds = dscore.astype(jnp.bfloat16)
        ds_low[slot] = ds
        key_part = dot(ds, q_all[...].reshape(queries, width), 1, 0) * scale
        points = -to_row(jnp.sum(dscore, axis=1, keepdims=True))
        if isinstance(slot, int):
            pts_out[slot : slot + 1, :] = points
        else:
            pts_out[pl.ds(slot, 1), :] = points
        if isinstance(slot, int) and slot == 0:
            dk_ref[...] = key_part
        else:
            dk_out[slot] = key_part.astype(jnp.bfloat16)
            column_out(0, slot).start()

    for_each(rows - 1, lambda i: second_pass(i + 1))
    second_pass(0)
    value_pass(0)

    def pts_copy(shift):
        return pltpu.make_async_remote_copy(
            src_ref=pts_out,
            dst_ref=pts_in.at[me],
            send_sem=pts_send.at[shift],
            recv_sem=pts_recv.at[shift],
            device_id=at(other(shift)),
            device_id_type=MESH,
        )

    def pts_arrival(shift):
        source = lax.rem(me + devices - shift, devices)
        return pltpu.make_async_remote_copy(
            src_ref=pts_out,
            dst_ref=pts_in.at[source],
            send_sem=pts_send.at[shift],
            recv_sem=pts_recv.at[shift],
            device_id=at(other(shift)),
            device_id_type=MESH,
        )

    lax.fori_loop(1, devices, lambda i, c: (pts_copy(i).start(), c)[1], 0)
    pts_in[pl.ds(me, 1)] = pts_out[...].reshape(1, *pts_out.shape)

    ds_flat = ds_low[...].reshape(rows * tokens, queries)
    k_flat = k_all[...].reshape(rows * tokens, width)
    query_part = dot(k_flat, ds_flat, 0, 0) * scale
    for slot in range(1, cols):
        dq_out[slot] = query_part[:, slot * tokens : (slot + 1) * tokens].astype(jnp.bfloat16)
        row_out(1, slot).start()

    for slot in range(1, cols):
        row_out(0, cols - slot).wait_recv()
    out_sum = out_part[:, :tokens]
    for slot in range(1, cols):
        out_sum = out_sum + o_in[slot].astype(jnp.float32)
    out_ref[...] = jnp.transpose(out_sum).astype(out_ref.dtype)

    lax.fori_loop(1, devices, lambda i, c: (pts_arrival(i).wait_recv(), c)[1], 0)

    def add_points(index, carry):
        later, own = carry
        row = index // cols
        col = index % cols
        point = jnp.zeros((1, tokens), jnp.float32)
        for s in range(rows):
            giver = lax.rem(row + rows - s, rows) * cols + col
            point = point + pts_in[giver, s : s + 1, :]
        their_order = meta[index, 1:2, :]
        for half in range(halves):
            later[half] = later[half] + jnp.where(
                their_order > order_ref[half].astype(jnp.float32), point, 0.0
            )
        return (later, jnp.where(index == me, point, own))

    carry = ([jnp.zeros((1, tokens), jnp.float32) for _ in range(halves)],) + (
        jnp.zeros((1, tokens), jnp.float32),
    )
    if devices <= 16:
        for index in range(devices):
            carry = add_points(index, carry)
    else:
        carry = lax.fori_loop(0, devices, add_points, carry)
    later, own = carry
    gate_grad = jnp.sum(jnp.where(same & (line >= lane), to_column(own), 0.0), axis=0, keepdims=True)
    for half in range(halves):
        rest = jnp.sum(later[half], axis=1, keepdims=True)
        gate_grad = jnp.where(lane_row // piece == half, gate_grad + rest, gate_grad)
    dgate_ref[...] = gate_grad.reshape(tokens)

    for slot in range(1, cols):
        row_out(1, cols - slot).wait_recv()
    query_sum = query_part[:, :tokens]
    for slot in range(1, cols):
        query_sum = query_sum + dq_in[slot].astype(jnp.float32)
    dq_ref[...] = jnp.transpose(query_sum)

    for which, target in enumerate((dk_ref, dv_ref)):
        for slot in range(1, rows):
            column_out(which, rows - slot).wait_recv()
        for slot in range(1, rows):
            target[...] += (dk_in, dv_in)[which][slot].astype(jnp.float32)

    lax.fori_loop(1, devices, lambda i, c: (meta_copy(i).wait_send(), c)[1], 0)
    lax.fori_loop(1, devices, lambda i, c: (pts_copy(i).wait_send(), c)[1], 0)
    for which in range(2):
        for shift in range(1, cols):
            row_copy(which, shift).wait_send()
            row_out(which, shift).wait_send()
        for shift in range(1, rows):
            column_copy(which, shift).wait_send()
            column_out(which, shift).wait_send()
    for shift in range(1, cols):
        stat_copy(shift).wait_send()
        delta_copy(shift).wait_send()


def hand_on(count, *refs):
    sources, targets, sems = refs[:count], refs[count : 2 * count], refs[2 * count]
    copies = [
        pltpu.make_async_copy(source, target, sems.at[index])
        for index, (source, target) in enumerate(zip(sources, targets))
    ]
    for copy in copies:
        copy.start()
    for copy in copies:
        copy.wait()


def local(rows, cols, queries, keys, values, log_gate, out_grad, segment_order):
    tokens, width = queries.shape
    halves = segment_order.shape[0]
    devices = rows * cols
    across = cols * tokens
    low, full = jnp.bfloat16, jnp.float32
    dma = pltpu.SemaphoreType.DMA
    in_vmem = pl.BlockSpec(memory_space=pltpu.VMEM)
    in_hbm = pl.BlockSpec(memory_space=pltpu.HBM)
    shapes = (
        jax.ShapeDtypeStruct((tokens, width), low),
        jax.ShapeDtypeStruct((tokens, width), full),
        jax.ShapeDtypeStruct((tokens, width), full),
        jax.ShapeDtypeStruct((tokens, width), full),
        jax.ShapeDtypeStruct((tokens,), full),
    )
    results = pl.pallas_call(
        functools.partial(kernel, rows, cols, halves),
        out_shape=tuple(pltpu.VMEM(shape.shape, shape.dtype) for shape in shapes),
        in_specs=[in_hbm] * 5 + [pl.BlockSpec(memory_space=pltpu.SMEM)],
        out_specs=[in_vmem] * 5,
        scratch_shapes=[
            pltpu.VMEM((tokens,), full),
            dma((5,)),
            pltpu.VMEM((devices, 2, tokens), full),
            pltpu.VMEM((rows, tokens), full),
            pltpu.VMEM((devices, rows, tokens), full),
            pltpu.VMEM((devices, tokens), full),
            pltpu.VMEM((devices, tokens), full),
            pltpu.VMEM((cols, tokens, width), low),
            pltpu.VMEM((cols, tokens, width), low),
            pltpu.VMEM((rows, tokens, width), low),
            pltpu.VMEM((rows, tokens, width), low),
            pltpu.VMEM((rows, tokens, across), full),
            pltpu.VMEM((rows, tokens, across), full),
            pltpu.VMEM((rows, 8, across), full),
            pltpu.VMEM((cols, 4, across), full),
            pltpu.VMEM((cols, 1, across), full),
            pltpu.VMEM((rows, tokens, across), low),
            pltpu.VMEM((rows, tokens, across), low),
            pltpu.VMEM((rows, tokens, width), low),
            pltpu.VMEM((rows, tokens, width), low),
            pltpu.VMEM((rows, tokens, width), low),
            pltpu.VMEM((rows, tokens, width), low),
            pltpu.VMEM((cols, tokens, width), low),
            pltpu.VMEM((cols, tokens, width), low),
            pltpu.VMEM((cols, tokens, width), low),
            pltpu.VMEM((cols, tokens, width), low),
            dma((devices,)),
            dma((devices,)),
            dma((devices,)),
            dma((devices,)),
            dma((2, cols)),
            dma((2, cols)),
            dma((2, rows)),
            dma((2, rows)),
            dma((cols,)),
            dma((cols,)),
            dma((cols,)),
            dma((cols,)),
            dma((2, rows)),
            dma((2, rows)),
            dma((2, cols)),
            dma((2, cols)),
        ],
        compiler_params=pltpu.CompilerParams(
            collective_id=0, has_side_effects=True, vmem_limit_bytes=60 * 1024 * 1024
        ),
    )(queries, keys, values, log_gate, out_grad, segment_order)
    return pl.pallas_call(
        functools.partial(hand_on, len(shapes)),
        out_shape=shapes,
        in_specs=[in_vmem] * len(shapes),
        out_specs=[in_hbm] * len(shapes),
        scratch_shapes=[dma((len(shapes),))],
    )(*results)


def solution(mesh):
    devices = mesh.shape["seq"]
    cols = max(c for c in range(1, math.isqrt(devices) + 1) if devices % c == 0)
    flat = P(("grp", "seq"))
    wide = P(("grp", "seq"), None)
    return jax.shard_map(
        functools.partial(local, devices // cols, cols),
        mesh=mesh,
        in_specs=(wide, wide, wide, flat, wide, flat),
        out_specs=(wide, wide, wide, wide, flat),
        check_vma=False,
    )
```

time: 212 us -> 32.5 us (0.15)
  blocking collectives: 197 us -> 0 us
  Pallas kernels: 0 us -> 28.6 us
  matrix products: 5.38 us -> 0 us
  local copies, waits for them, and re-layouts: 5.65 us -> 3.04 us
    all_gather x7 -> x0, blocking collectives: 137 us -> none  [the longest x1 24.6 us: local(): lax.all_gather(values, 'seq', axis=0, tiled=True)]
    unnamed x2 -> x0, blocking collectives: 59.6 us -> none
    pallas_call x0 -> x2, Pallas kernels: none -> 28.6 us  [the longest x1 26.9 us: local(): pl.pallas_call(functools.partial(kernel, rows, cols, halves), out_shape=t...]
    dot_general x7 -> x0, matrix products: 5.38 us -> none  [the longest x2 1.95 us: contract_first(): lax.dot_general(left, right, (((0,), (0,)), ((), ())), preferred_element_...]
where the time goes in v1:
time: 32.5 us; the launch traced here: 32.2 us
  Pallas kernels  28.6 us (88%)
  local copies, waits for them, and re-layouts  3.04 us (9%)
  between operations  0.65 us (2%)
    pallas_call x1, Pallas kernels, local(): pl.pallas_call(functools.partial(kernel, rows, cols, halves), out_shape=t...  26.9 us
    unnamed x10, local copies, waits for them, and re-layouts  3.04 us
    pallas_call x1, Pallas kernels, local(): pl.pallas_call(functools.partial(hand_on, len(shapes)), out_shape=shapes,...  1.65 us

profile of v1, /device:TPU:0, one launch (start us, length us, event | category | flops | bytes accessed | tf_op | source)
XLA Modules:
  0.0 32.2 jit_solution(15515151124352774362)
XLA Ops:
  0.6 26.9 %shard_map.101 = (bf16[128,128]{1,0:T(8,128)(2,1)S(1)}, f32[128,128]{1,0:T(8,128)S(1)}, f32[128,128]{1,0:T(8,128)S(1)}, f32[128,128]{1,0:T(8,128)S(1)}, f32[128]{0:T(128)S(1)}) custom-call(bf16[128,128]{1,0:T(8,128)(2,1)} %q_hbm.1, bf16[128,128]{1,0:T(8,128)(2,1)} %k_hbm.1, bf16[128,128]{1,0:T(8,128)(2,1)} %v_hbm.1, f32[128]{0:T(128)} %gate_hbm.1, ...), custom_call_target="tpu_custom_call" | custom-call | tf_op jit(solution)/shard_map/pallas_call | solution.py:521
  27.5 0.0 copy-start
  27.6 0.6 %copy-done = f32[128,128]{1,0:T(8,128)} copy-done((f32[128,128]{1,0:T(8,128)}, f32[128,128]{1,0:T(8,128)S(1)}, u32[]{:S(2)}) %copy-start) | copy-done | bytes 65560
  28.2 0.0 copy-start.1
  28.2 0.6 %copy-done.1 = f32[128,128]{1,0:T(8,128)} copy-done((f32[128,128]{1,0:T(8,128)}, f32[128,128]{1,0:T(8,128)S(1)}, u32[]{:S(2)}) %copy-start.1) | copy-done | bytes 65560
  28.8 0.0 copy-start.2
  28.8 0.6 %copy-done.2 = f32[128,128]{1,0:T(8,128)} copy-done((f32[128,128]{1,0:T(8,128)}, f32[128,128]{1,0:T(8,128)S(1)}, u32[]{:S(2)}) %copy-start.2) | copy-done | bytes 65560
  29.4 0.0 copy-start.3
  29.4 0.6 %copy-done.3 = bf16[128,128]{1,0:T(8,128)(2,1)} copy-done((bf16[128,128]{1,0:T(8,128)(2,1)}, bf16[128,128]{1,0:T(8,128)(2,1)S(1)}, u32[]{:S(2)}) %copy-start.3) | copy-done | bytes 32792
  30.0 0.0 copy-start.4
  30.0 0.6 %copy-done.4 = f32[128]{0:T(128)} copy-done((f32[128]{0:T(128)}, f32[128]{0:T(128)S(1)}, u32[]{:S(2)}) %copy-start.4) | copy-done | bytes 536
  30.6 1.6 %shard_map.102 = (bf16[128,128]{1,0:T(8,128)(2,1)}, f32[128,128]{1,0:T(8,128)}, f32[128,128]{1,0:T(8,128)}, f32[128,128]{1,0:T(8,128)}, f32[128]{0:T(128)}) custom-call(bf16[128,128]{1,0:T(8,128)(2,1)} %copy-done.3, f32[128,128]{1,0:T(8,128)} %copy-done, f32[128,128]{1,0:T(8,128)} %copy-done.1, f32[128,128]{1,0:T(8,128)} %copy-done.2, f32[128]{0:T(128)} %copy-done.4), custom_call_target="tpu_custom_call" | custom-call | tf_op jit(solution)/shard_map/pallas_call | solution.py:574
Async XLA Ops:
  27.5 0.6 %copy-start = (f32[128,128]{1,0:T(8,128)}, f32[128,128]{1,0:T(8,128)S(1)}, u32[]{:S(2)}) copy-start(f32[128,128]{1,0:T(8,128)S(1)} %get-tuple-element.11.refs_1_) | copy-start | bytes 196612
  28.2 0.6 %copy-start.1 = (f32[128,128]{1,0:T(8,128)}, f32[128,128]{1,0:T(8,128)S(1)}, u32[]{:S(2)}) copy-start(f32[128,128]{1,0:T(8,128)S(1)} %get-tuple-element.12.refs_2_) | copy-start | bytes 196612
  28.8 0.6 %copy-start.2 = (f32[128,128]{1,0:T(8,128)}, f32[128,128]{1,0:T(8,128)S(1)}, u32[]{:S(2)}) copy-start(f32[128,128]{1,0:T(8,128)S(1)} %get-tuple-element.13.refs_3_) | copy-start | bytes 196612
  29.4 0.6 %copy-start.3 = (bf16[128,128]{1,0:T(8,128)(2,1)}, bf16[128,128]{1,0:T(8,128)(2,1)S(1)}, u32[]{:S(2)}) copy-start(bf16[128,128]{1,0:T(8,128)(2,1)S(1)} %get-tuple-element.10.refs_0_) | copy-start | bytes 98308
  30.0 0.6 %copy-start.4 = (f32[128]{0:T(128)}, f32[128]{0:T(128)S(1)}, u32[]{:S(2)}) copy-start(f32[128]{0:T(128)S(1)} %get-tuple-element.14.refs_4_) | copy-start | bytes 1540

commit v2 on v1

--- a/solution.py
+++ b/solution.py
@@ -46,7 +46,6 @@
     gate_ref,
     load_sems,
     meta,
-    pts_out,
     pts_in,
     cum,
     place,
@@ -102,6 +101,13 @@
     def other(shift):
         return lax.rem(me + shift, devices)
 
+    def slot_of(index):
+        return lax.rem(me + devices - index, devices)
+
+    def arrive(slots, sem):
+        rest = slots.at[pl.ds(1, slots.shape[0] - 1)]
+        pltpu.make_async_copy(rest, rest, sem).wait()
+
     def in_row(shift):
         return my_row * cols + lax.rem(my_col + shift, cols)
 
@@ -153,8 +159,8 @@
         own_order = jnp.where(
             lane_row // piece == half, order_ref[half].astype(jnp.float32), own_order
         )
-    meta[pl.ds(me, 1), 0:1, :] = local_cum.reshape(1, 1, tokens)
-    meta[pl.ds(me, 1), 1:2, :] = own_order.reshape(1, 1, tokens)
+    meta[0, 0:1, :] = local_cum
+    meta[0, 1:2, :] = own_order
     for load in loads[1:]:
         load.wait()
 
@@ -162,21 +168,10 @@
 
     def meta_copy(shift):
         return pltpu.make_async_remote_copy(
-            src_ref=meta.at[me],
-            dst_ref=meta.at[me],
-            send_sem=meta_send.at[shift],
-            recv_sem=meta_recv.at[shift],
-            device_id=at(other(shift)),
-            device_id_type=MESH,
-        )
-
-    def meta_arrival(shift):
-        source = lax.rem(me + devices - shift, devices)
-        return pltpu.make_async_remote_copy(
-            src_ref=meta.at[source],
-            dst_ref=meta.at[source],
-            send_sem=meta_send.at[shift],
-            recv_sem=meta_recv.at[shift],
+            src_ref=meta.at[0],
+            dst_ref=meta.at[shift],
+            send_sem=meta_send,
+            recv_sem=meta_recv,
             device_id=at(other(shift)),
             device_id_type=MESH,
         )
@@ -186,8 +181,8 @@
         return pltpu.make_async_remote_copy(
             src_ref=ref,
             dst_ref=slots.at[cols - shift],
-            send_sem=q_send.at[which, shift],
-            recv_sem=q_recv.at[which, cols - shift],
+            send_sem=q_send.at[which],
+            recv_sem=q_recv.at[which],
             device_id=at(in_row(shift)),
             device_id_type=MESH,
         )
@@ -197,20 +192,23 @@
         return pltpu.make_async_remote_copy(
             src_ref=ref,
             dst_ref=slots.at[rows - shift],
-            send_sem=k_send.at[which, shift],
+            send_sem=k_send.at[which],
             recv_sem=k_recv.at[which, rows - shift],
             device_id=at(in_column(shift)),
             device_id_type=MESH,
         )
 
+    for shift in range(1, rows):
+        column_copy(0, shift).start()
+    for shift in range(1, cols):
+        row_copy(0, shift).start()
     lax.fori_loop(1, devices, lambda i, c: (meta_copy(i).start(), c)[1], 0)
-    for which in range(2):
-        for shift in range(1, cols):
-            row_copy(which, shift).start()
-        for shift in range(1, rows):
-            column_copy(which, shift).start()
-
-    lax.fori_loop(1, devices, lambda i, c: (meta_arrival(i).wait_recv(), c)[1], 0)
+    for shift in range(1, rows):
+        column_copy(1, shift).start()
+    for shift in range(1, cols):
+        row_copy(1, shift).start()
+
+    arrive(meta, meta_recv)
 
     orders = meta[:, 1, :]
     base = meta[:, 0, :]
@@ -226,14 +224,13 @@
     within = (lax.broadcasted_iota(jnp.int32, (devices, tokens), 1) % piece).astype(jnp.float32)
     place[...] = orders * piece + within
 
-    query_cum = jnp.concatenate([cum[pl.ds(in_row(s), 1), :] for s in range(cols)], axis=1)
-    query_place = jnp.concatenate([place[pl.ds(in_row(s), 1), :] for s in range(cols)], axis=1)
-
-    for shift in range(1, cols):
-        row_copy(0, cols - shift).wait_recv()
+    query_cum = jnp.concatenate([cum[pl.ds(slot_of(in_row(s)), 1), :] for s in range(cols)], axis=1)
+    query_place = jnp.concatenate([place[pl.ds(slot_of(in_row(s)), 1), :] for s in range(cols)], axis=1)
+
+    arrive(q_all, q_recv.at[0])
 
     def first_pass(slot):
-        source = in_column(slot)
+        source = slot_of(in_column(slot))
         key_cum = to_column(cum[pl.ds(source, 1), :])
         key_place = to_column(place[pl.ds(source, 1), :])
         if isinstance(slot, int) and slot == 0:
@@ -254,7 +251,7 @@
         pltpu.make_async_remote_copy(
             src_ref=ref,
             dst_ref=slots.at[slot],
-            send_sem=k_send.at[which, slot],
+            send_sem=k_send.at[which],
             recv_sem=k_recv.at[which, slot],
             device_id=at(in_column(slot)),
             device_id_type=MESH,
@@ -273,8 +270,8 @@
         return pltpu.make_async_remote_copy(
             src_ref=stats.at[0],
             dst_ref=stats.at[cols - shift],
-            send_sem=stat_send.at[shift],
-            recv_sem=stat_recv.at[cols - shift],
+            send_sem=stat_send,
+            recv_sem=stat_recv,
             device_id=at(in_row(shift)),
             device_id_type=MESH,
         )
@@ -282,10 +279,8 @@
     for shift in range(1, cols):
         stat_copy(shift).start()
 
-    for shift in range(1, cols):
-        row_copy(1, cols - shift).wait_recv()
-    for shift in range(1, cols):
-        stat_copy(cols - shift).wait_recv()
+    arrive(g_all, q_recv.at[1])
+    arrive(stats, stat_recv)
 
     def turn(turned, slot):
         cut = (cols - slot) * tokens
@@ -319,8 +314,8 @@
         return pltpu.make_async_remote_copy(
             src_ref=deltas.at[0],
             dst_ref=deltas.at[cols - shift],
-            send_sem=delta_send.at[shift],
-            recv_sem=delta_recv.at[cols - shift],
+            send_sem=delta_send,
+            recv_sem=delta_recv,
             device_id=at(in_row(shift)),
             device_id_type=MESH,
         )
@@ -333,8 +328,8 @@
         return pltpu.make_async_remote_copy(
             src_ref=source.at[slot],
             dst_ref=target.at[rows - slot],
-            send_sem=kout_send.at[which, slot],
-            recv_sem=kout_recv.at[which, rows - slot],
+            send_sem=kout_send.at[which],
+            recv_sem=kout_recv.at[which],
             device_id=at(in_column(slot)),
             device_id_type=MESH,
         )
@@ -354,8 +349,8 @@
         return pltpu.make_async_remote_copy(
             src_ref=source.at[slot],
             dst_ref=target.at[cols - slot],
-            send_sem=qout_send.at[which, slot],
-            recv_sem=qout_recv.at[which, cols - slot],
+            send_sem=qout_send.at[which],
+            recv_sem=qout_recv.at[which],
             device_id=at(in_row(slot)),
             device_id_type=MESH,
         )
@@ -367,8 +362,7 @@
         o_out[slot] = out_part[:, slot * tokens : (slot + 1) * tokens].astype(jnp.bfloat16)
         row_out(0, slot).start()
 
-    for shift in range(1, cols):
-        delta_copy(cols - shift).wait_recv()
+    arrive(deltas, delta_recv)
     delta = deltas[0]
     for slot in range(1, cols):
         delta = delta + turn(deltas[slot], slot)
@@ -380,9 +374,9 @@
         key_part = dot(ds, q_all[...].reshape(queries, width), 1, 0) * scale
         points = -to_row(jnp.sum(dscore, axis=1, keepdims=True))
         if isinstance(slot, int):
-            pts_out[slot : slot + 1, :] = points
+            pts_in[0, slot : slot + 1, :] = points
         else:
-            pts_out[pl.ds(slot, 1), :] = points
+            pts_in[0, pl.ds(slot, 1), :] = points
         if isinstance(slot, int) and slot == 0:
             dk_ref[...] = key_part
         else:
@@ -395,27 +389,15 @@
 
     def pts_copy(shift):
         return pltpu.make_async_remote_copy(
-            src_ref=pts_out,
-            dst_ref=pts_in.at[me],
-            send_sem=pts_send.at[shift],
-            recv_sem=pts_recv.at[shift],
+            src_ref=pts_in.at[0],
+            dst_ref=pts_in.at[shift],
+            send_sem=pts_send,
+            recv_sem=pts_recv,
             device_id=at(other(shift)),
             device_id_type=MESH,
         )
 
-    def pts_arrival(shift):
-        source = lax.rem(me + devices - shift, devices)
-        return pltpu.make_async_remote_copy(
-            src_ref=pts_out,
-            dst_ref=pts_in.at[source],
-            send_sem=pts_send.at[shift],
-            recv_sem=pts_recv.at[shift],
-            device_id=at(other(shift)),
-            device_id_type=MESH,
-        )
-
     lax.fori_loop(1, devices, lambda i, c: (pts_copy(i).start(), c)[1], 0)
-    pts_in[pl.ds(me, 1)] = pts_out[...].reshape(1, *pts_out.shape)
 
     ds_flat = ds_low[...].reshape(rows * tokens, queries)
     k_flat = k_all[...].reshape(rows * tokens, width)
@@ -424,14 +406,13 @@
         dq_out[slot] = query_part[:, slot * tokens : (slot + 1) * tokens].astype(jnp.bfloat16)
         row_out(1, slot).start()
 
-    for slot in range(1, cols):
-        row_out(0, cols - slot).wait_recv()
+    arrive(o_in, qout_recv.at[0])
     out_sum = out_part[:, :tokens]
     for slot in range(1, cols):
         out_sum = out_sum + o_in[slot].astype(jnp.float32)
     out_ref[...] = jnp.transpose(out_sum).astype(out_ref.dtype)
 
-    lax.fori_loop(1, devices, lambda i, c: (pts_arrival(i).wait_recv(), c)[1], 0)
+    arrive(pts_in, pts_recv)
 
     def add_points(index, carry):
         later, own = carry
@@ -440,8 +421,8 @@
         point = jnp.zeros((1, tokens), jnp.float32)
         for s in range(rows):
             giver = lax.rem(row + rows - s, rows) * cols + col
-            point = point + pts_in[giver, s : s + 1, :]
-        their_order = meta[index, 1:2, :]
+            point = point + pts_in[slot_of(giver), s : s + 1, :]
+        their_order = meta[slot_of(index), 1:2, :]
         for half in range(halves):
             later[half] = later[half] + jnp.where(
                 their_order > order_ref[half].astype(jnp.float32), point, 0.0
@@ -463,31 +444,26 @@
         gate_grad = jnp.where(lane_row // piece == half, gate_grad + rest, gate_grad)
     dgate_ref[...] = gate_grad.reshape(tokens)
 
-    for slot in range(1, cols):
-        row_out(1, cols - slot).wait_recv()
+    arrive(dq_in, qout_recv.at[1])
     query_sum = query_part[:, :tokens]
     for slot in range(1, cols):
         query_sum = query_sum + dq_in[slot].astype(jnp.float32)
     dq_ref[...] = jnp.transpose(query_sum)
 
     for which, target in enumerate((dk_ref, dv_ref)):
-        for slot in range(1, rows):
-            column_out(which, rows - slot).wait_recv()
+        arrive((dk_in, dv_in)[which], kout_recv.at[which])
         for slot in range(1, rows):
             target[...] += (dk_in, dv_in)[which][slot].astype(jnp.float32)
 
-    lax.fori_loop(1, devices, lambda i, c: (meta_copy(i).wait_send(), c)[1], 0)
-    lax.fori_loop(1, devices, lambda i, c: (pts_copy(i).wait_send(), c)[1], 0)
+    arrive(meta, meta_send)
+    arrive(pts_in, pts_send)
+    arrive(stats, stat_send)
+    arrive(deltas, delta_send)
     for which in range(2):
-        for shift in range(1, cols):
-            row_copy(which, shift).wait_send()
-            row_out(which, shift).wait_send()
-        for shift in range(1, rows):
-            column_copy(which, shift).wait_send()
-            column_out(which, shift).wait_send()
-    for shift in range(1, cols):
-        stat_copy(shift).wait_send()
-        delta_copy(shift).wait_send()
+        arrive(q_all, q_send.at[which])
+        arrive(k_all, k_send.at[which])
+        arrive(o_in, qout_send.at[which])
+        arrive(dk_in, kout_send.at[which])
 
 
 def hand_on(count, *refs):
@@ -527,7 +503,6 @@
             pltpu.VMEM((tokens,), full),
             dma((5,)),
             pltpu.VMEM((devices, 2, tokens), full),
-            pltpu.VMEM((rows, tokens), full),
             pltpu.VMEM((devices, rows, tokens), full),
             pltpu.VMEM((devices, tokens), full),
             pltpu.VMEM((devices, tokens), full),
@@ -550,22 +525,22 @@
             pltpu.VMEM((cols, tokens, width), low),
             pltpu.VMEM((cols, tokens, width), low),
             pltpu.VMEM((cols, tokens, width), low),
-            dma((devices,)),
-            dma((devices,)),
-            dma((devices,)),
-            dma((devices,)),
-            dma((2, cols)),
-            dma((2, cols)),
+            dma(()),
+            dma(()),
+            dma(()),
+            dma(()),
+            dma((2,)),
+            dma((2,)),
+            dma((2,)),
             dma((2, rows)),
-            dma((2, rows)),
-            dma((cols,)),
-            dma((cols,)),
-            dma((cols,)),
-            dma((cols,)),
-            dma((2, rows)),
-            dma((2, rows)),
-            dma((2, cols)),
-            dma((2, cols)),
+            dma(()),
+            dma(()),
+            dma(()),
+            dma(()),
+            dma((2,)),
+            dma((2,)),
+            dma((2,)),
+            dma((2,)),
         ],
         compiler_params=pltpu.CompilerParams(
             collective_id=0, has_side_effects=True, vmem_limit_bytes=60 * 1024 * 1024
@@ -577,6 +552,7 @@
         in_specs=[in_vmem] * len(shapes),
         out_specs=[in_hbm] * len(shapes),
         scratch_shapes=[dma((len(shapes),))],
+        compiler_params=pltpu.CompilerParams(vmem_limit_bytes=1024 * 1024),
     )(*results)
 
 

time: 32.5 us -> 28.6 us (0.88)
  local copies, waits for them, and re-layouts: 3.04 us -> 0 us
  Pallas kernels: 28.6 us -> 27.7 us
    unnamed x10 -> x0, local copies, waits for them, and re-layouts: 3.04 us -> none
    pallas_call x1, Pallas kernels: 1.65 us -> 0.73 us  [local(): pl.pallas_call(functools.partial(hand_on, len(shapes)), out_shape=shapes,...]
where the time goes in v2:
time: 28.6 us; the launch traced here: 28.4 us
  Pallas kernels  27.7 us (97%)
  between operations  0.64 us (2%)
    pallas_call x1, Pallas kernels, local(): pl.pallas_call(functools.partial(kernel, rows, cols, halves), out_shape=t...  27 us
    pallas_call x1, Pallas kernels, local(): pl.pallas_call(functools.partial(hand_on, len(shapes)), out_shape=shapes,...  0.73 us

profile of v2, /device:TPU:0, one launch (start us, length us, event | category | flops | bytes accessed | tf_op | source)
XLA Modules:
  0.0 28.4 jit_solution(15168781865341866783)
XLA Ops:
  0.6 27.0 %shard_map.101 = (bf16[128,128]{1,0:T(8,128)(2,1)S(1)}, f32[128,128]{1,0:T(8,128)S(1)}, f32[128,128]{1,0:T(8,128)S(1)}, f32[128,128]{1,0:T(8,128)S(1)}, f32[128]{0:T(128)S(1)}) custom-call(bf16[128,128]{1,0:T(8,128)(2,1)} %q_hbm.1, bf16[128,128]{1,0:T(8,128)(2,1)} %k_hbm.1, bf16[128,128]{1,0:T(8,128)(2,1)} %v_hbm.1, f32[128]{0:T(128)} %gate_hbm.1, ...), custom_call_target="tpu_custom_call" | custom-call | tf_op jit(solution)/shard_map/pallas_call | solution.py:497
  27.7 0.7 %shard_map.102 = (bf16[128,128]{1,0:T(8,128)(2,1)}, f32[128,128]{1,0:T(8,128)}, f32[128,128]{1,0:T(8,128)}, f32[128,128]{1,0:T(8,128)}, f32[128]{0:T(128)}) custom-call(bf16[128,128]{1,0:T(8,128)(2,1)S(1)} %get-tuple-element.10.refs_0_, f32[128,128]{1,0:T(8,128)S(1)} %get-tuple-element.11.refs_1_, f32[128,128]{1,0:T(8,128)S(1)} %get-tuple-element.12.refs_2_, ...), custom_call_target="tpu_custom_call" | custom-call | tf_op jit(solution)/shard_map/pallas_call | solution.py:549

commit v3 on v2

--- a/solution.py
+++ b/solution.py
@@ -98,14 +98,8 @@
     def at(index):
         return (grp, index)
 
-    def other(shift):
-        return lax.rem(me + shift, devices)
-
-    def slot_of(index):
-        return lax.rem(me + devices - index, devices)
-
-    def arrive(slots, sem):
-        rest = slots.at[pl.ds(1, slots.shape[0] - 1)]
+    def arrive(slots, sem, first=1):
+        rest = slots.at[pl.ds(first, slots.shape[0] - first)]
         pltpu.make_async_copy(rest, rest, sem).wait()
 
     def in_row(shift):
@@ -116,10 +110,9 @@
 
     barrier = pltpu.get_barrier_semaphore()
 
-    def greet(shift):
-        pl.semaphore_signal(barrier, inc=1, device_id=at(other(shift + 1)), device_id_type=MESH)
-
-    lax.fori_loop(0, devices - 1, lambda i, c: (greet(i), c)[1], 0)
+    partners = [in_row(s) for s in range(1, cols)] + [in_column(s) for s in range(1, rows)]
+    for partner in partners:
+        pl.semaphore_signal(barrier, inc=1, device_id=at(partner), device_id_type=MESH)
 
     q_ref, g_ref, k_ref, v_ref = q_all.at[0], g_all.at[0], k_all.at[0], v_all.at[0]
     loads = [
@@ -164,15 +157,25 @@
     for load in loads[1:]:
         load.wait()
 
-    pl.semaphore_wait(barrier, devices - 1)
-
-    def meta_copy(shift):
+    pl.semaphore_wait(barrier, len(partners))
+
+    def meta_row_copy(shift):
         return pltpu.make_async_remote_copy(
             src_ref=meta.at[0],
-            dst_ref=meta.at[shift],
-            send_sem=meta_send,
-            recv_sem=meta_recv,
-            device_id=at(other(shift)),
+            dst_ref=meta.at[cols - shift],
+            send_sem=meta_send.at[0],
+            recv_sem=meta_recv.at[0],
+            device_id=at(in_row(shift)),
+            device_id_type=MESH,
+        )
+
+    def meta_column_copy(shift):
+        return pltpu.make_async_remote_copy(
+            src_ref=meta.at[pl.ds(0, cols)],
+            dst_ref=meta.at[pl.ds((rows - shift) * cols, cols)],
+            send_sem=meta_send.at[1],
+            recv_sem=meta_recv.at[1],
+            device_id=at(in_column(shift)),
             device_id_type=MESH,
         )
 
@@ -198,17 +201,23 @@
             device_id_type=MESH,
         )
 
+    for shift in range(1, cols):
+        meta_row_copy(shift).start()
     for shift in range(1, rows):
         column_copy(0, shift).start()
     for shift in range(1, cols):
         row_copy(0, shift).start()
-    lax.fori_loop(1, devices, lambda i, c: (meta_copy(i).start(), c)[1], 0)
+    pltpu.make_async_copy(
+        meta.at[pl.ds(1, cols - 1)], meta.at[pl.ds(1, cols - 1)], meta_recv.at[0]
+    ).wait()
+    for shift in range(1, rows):
+        meta_column_copy(shift).start()
     for shift in range(1, rows):
         column_copy(1, shift).start()
     for shift in range(1, cols):
         row_copy(1, shift).start()
 
-    arrive(meta, meta_recv)
+    arrive(meta, meta_recv.at[1], cols)
 
     orders = meta[:, 1, :]
     base = meta[:, 0, :]
@@ -224,13 +233,13 @@
     within = (lax.broadcasted_iota(jnp.int32, (devices, tokens), 1) % piece).astype(jnp.float32)
     place[...] = orders * piece + within
 
-    query_cum = jnp.concatenate([cum[pl.ds(slot_of(in_row(s)), 1), :] for s in range(cols)], axis=1)
-    query_place = jnp.concatenate([place[pl.ds(slot_of(in_row(s)), 1), :] for s in range(cols)], axis=1)
+    query_cum = jnp.concatenate([cum[s : s + 1, :] for s in range(cols)], axis=1)
+    query_place = jnp.concatenate([place[s : s + 1, :] for s in range(cols)], axis=1)
 
     arrive(q_all, q_recv.at[0])
 
     def first_pass(slot):
-        source = slot_of(in_column(slot))
+        source = slot * cols
         key_cum = to_column(cum[pl.ds(source, 1), :])
         key_place = to_column(place[pl.ds(source, 1), :])
         if isinstance(slot, int) and slot == 0:
@@ -387,17 +396,28 @@
     second_pass(0)
     value_pass(0)
 
-    def pts_copy(shift):
+    def pts_row_copy(shift):
         return pltpu.make_async_remote_copy(
             src_ref=pts_in.at[0],
-            dst_ref=pts_in.at[shift],
-            send_sem=pts_send,
-            recv_sem=pts_recv,
-            device_id=at(other(shift)),
-            device_id_type=MESH,
-        )
-
-    lax.fori_loop(1, devices, lambda i, c: (pts_copy(i).start(), c)[1], 0)
+            dst_ref=pts_in.at[cols - shift],
+            send_sem=pts_send.at[0],
+            recv_sem=pts_recv.at[0],
+            device_id=at(in_row(shift)),
+            device_id_type=MESH,
+        )
+
+    def pts_column_copy(shift):
+        return pltpu.make_async_remote_copy(
+            src_ref=pts_in.at[pl.ds(0, cols)],
+            dst_ref=pts_in.at[pl.ds((rows - shift) * cols, cols)],
+            send_sem=pts_send.at[1],
+            recv_sem=pts_recv.at[1],
+            device_id=at(in_column(shift)),
+            device_id_type=MESH,
+        )
+
+    for shift in range(1, cols):
+        pts_row_copy(shift).start()
 
     ds_flat = ds_low[...].reshape(rows * tokens, queries)
     k_flat = k_all[...].reshape(rows * tokens, width)
@@ -406,38 +426,40 @@
         dq_out[slot] = query_part[:, slot * tokens : (slot + 1) * tokens].astype(jnp.bfloat16)
         row_out(1, slot).start()
 
+    pltpu.make_async_copy(
+        pts_in.at[pl.ds(1, cols - 1)], pts_in.at[pl.ds(1, cols - 1)], pts_recv.at[0]
+    ).wait()
+    for shift in range(1, rows):
+        pts_column_copy(shift).start()
+
     arrive(o_in, qout_recv.at[0])
     out_sum = out_part[:, :tokens]
     for slot in range(1, cols):
         out_sum = out_sum + o_in[slot].astype(jnp.float32)
     out_ref[...] = jnp.transpose(out_sum).astype(out_ref.dtype)
 
-    arrive(pts_in, pts_recv)
-
-    def add_points(index, carry):
-        later, own = carry
-        row = index // cols
-        col = index % cols
-        point = jnp.zeros((1, tokens), jnp.float32)
-        for s in range(rows):
-            giver = lax.rem(row + rows - s, rows) * cols + col
-            point = point + pts_in[slot_of(giver), s : s + 1, :]
-        their_order = meta[slot_of(index), 1:2, :]
-        for half in range(halves):
-            later[half] = later[half] + jnp.where(
-                their_order > order_ref[half].astype(jnp.float32), point, 0.0
-            )
-        return (later, jnp.where(index == me, point, own))
-
-    carry = ([jnp.zeros((1, tokens), jnp.float32) for _ in range(halves)],) + (
-        jnp.zeros((1, tokens), jnp.float32),
-    )
-    if devices <= 16:
-        for index in range(devices):
-            carry = add_points(index, carry)
-    else:
-        carry = lax.fori_loop(0, devices, add_points, carry)
-    later, own = carry
+    arrive(pts_in, pts_recv.at[1], cols)
+
+    later = [jnp.zeros((1, tokens), jnp.float32) for _ in range(halves)]
+
+    def points_of(row, col):
+        return functools.reduce(
+            jnp.add,
+            [
+                pts_in[r * cols + col, (row - r) % rows : (row - r) % rows + 1, :]
+                for r in range(rows)
+            ],
+        )
+
+    own = points_of(0, 0)
+    for row in range(rows):
+        for col in range(cols):
+            point = own if row == col == 0 else points_of(row, col)
+            their_order = meta[row * cols + col, 1:2, :]
+            for half in range(halves):
+                later[half] = later[half] + jnp.where(
+                    their_order > order_ref[half].astype(jnp.float32), point, 0.0
+                )
     gate_grad = jnp.sum(jnp.where(same & (line >= lane), to_column(own), 0.0), axis=0, keepdims=True)
     for half in range(halves):
         rest = jnp.sum(later[half], axis=1, keepdims=True)
@@ -455,8 +477,10 @@
         for slot in range(1, rows):
             target[...] += (dk_in, dv_in)[which][slot].astype(jnp.float32)
 
-    arrive(meta, meta_send)
-    arrive(pts_in, pts_send)
+    for buffer, sems in ((meta, meta_send), (pts_in, pts_send)):
+        sent = buffer.at[pl.ds(1, cols - 1)]
+        pltpu.make_async_copy(sent, sent, sems.at[0]).wait()
+        arrive(buffer, sems.at[1], cols)
     arrive(stats, stat_send)
     arrive(deltas, delta_send)
     for which in range(2):
@@ -525,10 +549,10 @@
             pltpu.VMEM((cols, tokens, width), low),
             pltpu.VMEM((cols, tokens, width), low),
             pltpu.VMEM((cols, tokens, width), low),
-            dma(()),
-            dma(()),
-            dma(()),
-            dma(()),
+            dma((2,)),
+            dma((2,)),
+            dma((2,)),
+            dma((2,)),
             dma((2,)),
             dma((2,)),
             dma((2,)),

time: 28.6 us -> 28.6 us (level)
  no operation moved by 1% of the time
where the time goes in v3:
time: 28.6 us; the launch traced here: 28.4 us
  Pallas kernels  27.7 us (97%)
  between operations  0.64 us (2%)
    pallas_call x1, Pallas kernels, local(): pl.pallas_call(functools.partial(kernel, rows, cols, halves), out_shape=t...  27 us
    pallas_call x1, Pallas kernels, local(): pl.pallas_call(functools.partial(hand_on, len(shapes)), out_shape=shapes,...  0.73 us

profile of v3, /device:TPU:0, one launch (start us, length us, event | category | flops | bytes accessed | tf_op | source)
XLA Modules:
  0.0 28.4 jit_solution(922263195260771542)
XLA Ops:
  0.6 27.0 %shard_map.101 = (bf16[128,128]{1,0:T(8,128)(2,1)S(1)}, f32[128,128]{1,0:T(8,128)S(1)}, f32[128,128]{1,0:T(8,128)S(1)}, f32[128,128]{1,0:T(8,128)S(1)}, f32[128]{0:T(128)S(1)}) custom-call(bf16[128,128]{1,0:T(8,128)(2,1)} %q_hbm.1, bf16[128,128]{1,0:T(8,128)(2,1)} %k_hbm.1, bf16[128,128]{1,0:T(8,128)(2,1)} %v_hbm.1, f32[128]{0:T(128)} %gate_hbm.1, ...), custom_call_target="tpu_custom_call" | custom-call | tf_op jit(solution)/shard_map/pallas_call | solution.py:521
  27.7 0.7 %shard_map.102 = (bf16[128,128]{1,0:T(8,128)(2,1)}, f32[128,128]{1,0:T(8,128)}, f32[128,128]{1,0:T(8,128)}, f32[128,128]{1,0:T(8,128)}, f32[128]{0:T(128)}) custom-call(bf16[128,128]{1,0:T(8,128)(2,1)S(1)} %get-tuple-element.10.refs_0_, f32[128,128]{1,0:T(8,128)S(1)} %get-tuple-element.11.refs_1_, f32[128,128]{1,0:T(8,128)S(1)} %get-tuple-element.12.refs_2_, ...), custom_call_target="tpu_custom_call" | custom-call | tf_op jit(solution)/shard_map/pallas_call | solution.py:573

commit v4 on v3

--- a/solution.py
+++ b/solution.py
@@ -289,6 +289,7 @@
         stat_copy(shift).start()
 
     arrive(g_all, q_recv.at[1])
+    dp_all[0] = dot(v_all[0], g_all[...].reshape(queries, width), 1, 1)
     arrive(stats, stat_recv)
 
     def turn(turned, slot):
@@ -302,36 +303,6 @@
     )
     inverse = 1.0 / sums
 
-    def normalise(slot):
-        if not (isinstance(slot, int) and slot == 0):
-            arrived(1, slot)
-        dprobs = dot(v_all[slot], g_all[...].reshape(queries, width), 1, 1)
-        probs = p_all[slot] * (jnp.exp2(part_stat[slot, 0:1, :] - top) * inverse)
-        low = probs.astype(jnp.bfloat16)
-        p_all[slot] = probs
-        p_low[slot] = low
-        dp_all[slot] = dprobs
-        part_stat[slot, 2:3, :] = jnp.sum(
-            low.astype(jnp.float32) * dprobs, axis=0, keepdims=True
-        )
-
-    normalise(0)
-    for_each(rows - 1, lambda i: normalise(i + 1))
-    deltas[0] = jnp.sum(part_stat[:, 2, :], axis=0, keepdims=True)
-
-    def delta_copy(shift):
-        return pltpu.make_async_remote_copy(
-            src_ref=deltas.at[0],
-            dst_ref=deltas.at[cols - shift],
-            send_sem=delta_send,
-            recv_sem=delta_recv,
-            device_id=at(in_row(shift)),
-            device_id_type=MESH,
-        )
-
-    for shift in range(1, cols):
-        delta_copy(shift).start()
-
     def column_out(which, slot):
         source, target = ((dk_out, dk_in), (dv_out, dv_in))[which]
         return pltpu.make_async_remote_copy(
@@ -342,6 +313,12 @@
             device_id=at(in_column(slot)),
             device_id_type=MESH,
         )
+
+    def normalise(slot):
+        probs = p_all[slot] * (jnp.exp2(part_stat[slot, 0:1, :] - top) * inverse)
+        low = probs.astype(jnp.bfloat16)
+        p_all[slot] = probs
+        p_low[slot] = low
 
     def value_pass(slot):
         value_part = dot(p_low[slot], g_all[...].reshape(queries, width), 1, 0)
@@ -351,7 +328,40 @@
             dv_out[slot] = value_part.astype(jnp.bfloat16)
             column_out(1, slot).start()
 
-    for_each(rows - 1, lambda i: value_pass(i + 1))
+    def remote_values(slot):
+        normalise(slot)
+        value_pass(slot)
+
+    for_each(rows - 1, lambda i: remote_values(i + 1))
+    normalise(0)
+
+    def delta_pass(slot):
+        if isinstance(slot, int) and slot == 0:
+            dprobs = dp_all[0]
+        else:
+            arrived(1, slot)
+            dprobs = dot(v_all[slot], g_all[...].reshape(queries, width), 1, 1)
+            dp_all[slot] = dprobs
+        part_stat[slot, 2:3, :] = jnp.sum(
+            p_low[slot].astype(jnp.float32) * dprobs, axis=0, keepdims=True
+        )
+
+    delta_pass(0)
+    for_each(rows - 1, lambda i: delta_pass(i + 1))
+    deltas[0] = jnp.sum(part_stat[:, 2, :], axis=0, keepdims=True)
+
+    def delta_copy(shift):
+        return pltpu.make_async_remote_copy(
+            src_ref=deltas.at[0],
+            dst_ref=deltas.at[cols - shift],
+            send_sem=delta_send,
+            recv_sem=delta_recv,
+            device_id=at(in_row(shift)),
+            device_id_type=MESH,
+        )
+
+    for shift in range(1, cols):
+        delta_copy(shift).start()
 
     def row_out(which, slot):
         source, target = ((o_out, o_in), (dq_out, dq_in))[which]
@@ -371,6 +381,7 @@
         o_out[slot] = out_part[:, slot * tokens : (slot + 1) * tokens].astype(jnp.bfloat16)
         row_out(0, slot).start()
 
+    value_pass(0)
     arrive(deltas, delta_recv)
     delta = deltas[0]
     for slot in range(1, cols):
@@ -394,7 +405,6 @@
 
     for_each(rows - 1, lambda i: second_pass(i + 1))
     second_pass(0)
-    value_pass(0)
 
     def pts_row_copy(shift):
         return pltpu.make_async_remote_copy(
@@ -472,7 +482,7 @@
         query_sum = query_sum + dq_in[slot].astype(jnp.float32)
     dq_ref[...] = jnp.transpose(query_sum)
 
-    for which, target in enumerate((dk_ref, dv_ref)):
+    for which, target in ((1, dv_ref), (0, dk_ref)):
         arrive((dk_in, dv_in)[which], kout_recv.at[which])
         for slot in range(1, rows):
             target[...] += (dk_in, dv_in)[which][slot].astype(jnp.float32)

time: 28.6 us -> 29 us (1.014)
  Pallas kernels: 27.7 us -> 28.2 us
    pallas_call x1, Pallas kernels: 27 us -> 27.5 us  [local(): pl.pallas_call(functools.partial(kernel, rows, cols, halves), out_shape=t...]
where the time goes in v4:
time: 29 us; the launch traced here: 28.8 us
  Pallas kernels  28.2 us (97%)
  between operations  0.64 us (2%)
    pallas_call x1, Pallas kernels, local(): pl.pallas_call(functools.partial(kernel, rows, cols, halves), out_shape=t...  27.5 us
    pallas_call x1, Pallas kernels, local(): pl.pallas_call(functools.partial(hand_on, len(shapes)), out_shape=shapes,...  0.73 us

profile of v4, /device:TPU:0, one launch (start us, length us, event | category | flops | bytes accessed | tf_op | source)
XLA Modules:
  0.0 28.8 jit_solution(12607792359922769667)
XLA Ops:
  0.6 27.5 %shard_map.101 = (bf16[128,128]{1,0:T(8,128)(2,1)S(1)}, f32[128,128]{1,0:T(8,128)S(1)}, f32[128,128]{1,0:T(8,128)S(1)}, f32[128,128]{1,0:T(8,128)S(1)}, f32[128]{0:T(128)S(1)}) custom-call(bf16[128,128]{1,0:T(8,128)(2,1)} %q_hbm.1, bf16[128,128]{1,0:T(8,128)(2,1)} %k_hbm.1, bf16[128,128]{1,0:T(8,128)(2,1)} %v_hbm.1, f32[128]{0:T(128)} %gate_hbm.1, ...), custom_call_target="tpu_custom_call" | custom-call | tf_op jit(solution)/shard_map/pallas_call | solution.py:531
  28.1 0.7 %shard_map.102 = (bf16[128,128]{1,0:T(8,128)(2,1)}, f32[128,128]{1,0:T(8,128)}, f32[128,128]{1,0:T(8,128)}, f32[128,128]{1,0:T(8,128)}, f32[128]{0:T(128)}) custom-call(bf16[128,128]{1,0:T(8,128)(2,1)S(1)} %get-tuple-element.10.refs_0_, f32[128,128]{1,0:T(8,128)S(1)} %get-tuple-element.11.refs_1_, f32[128,128]{1,0:T(8,128)S(1)} %get-tuple-element.12.refs_2_, ...), custom_call_target="tpu_custom_call" | custom-call | tf_op jit(solution)/shard_map/pallas_call | solution.py:583

commit v5 on v3

--- a/solution.py
+++ b/solution.py
@@ -224,8 +224,8 @@
     total = base
     for half in range(halves):
         totals = base[:, (half + 1) * piece - 1 : (half + 1) * piece]
-        heads = orders[:, half * piece : half * piece + 1]
-
+        totals = jnp.broadcast_to(totals, (devices, tokens))
+        heads = jnp.broadcast_to(orders[:, half * piece : half * piece + 1], (devices, tokens))
         for device in range(devices):
             earlier = heads[device : device + 1, :] < orders
             total = total + jnp.where(earlier, totals[device : device + 1, :], 0.0)
@@ -289,6 +289,7 @@
         stat_copy(shift).start()
 
     arrive(g_all, q_recv.at[1])
+    dp_all[0] = dot(v_all[0], g_all[...].reshape(queries, width), 1, 1)
     arrive(stats, stat_recv)
 
     def turn(turned, slot):
@@ -303,14 +304,16 @@
     inverse = 1.0 / sums
 
     def normalise(slot):
-        if not (isinstance(slot, int) and slot == 0):
+        if isinstance(slot, int) and slot == 0:
+            dprobs = dp_all[0]
+        else:
             arrived(1, slot)
-        dprobs = dot(v_all[slot], g_all[...].reshape(queries, width), 1, 1)
+            dprobs = dot(v_all[slot], g_all[...].reshape(queries, width), 1, 1)
+            dp_all[slot] = dprobs
         probs = p_all[slot] * (jnp.exp2(part_stat[slot, 0:1, :] - top) * inverse)
         low = probs.astype(jnp.bfloat16)
         p_all[slot] = probs
         p_low[slot] = low
-        dp_all[slot] = dprobs
         part_stat[slot, 2:3, :] = jnp.sum(
             low.astype(jnp.float32) * dprobs, axis=0, keepdims=True
         )
@@ -472,7 +475,7 @@
         query_sum = query_sum + dq_in[slot].astype(jnp.float32)
     dq_ref[...] = jnp.transpose(query_sum)
 
-    for which, target in enumerate((dk_ref, dv_ref)):
+    for which, target in ((1, dv_ref), (0, dk_ref)):
         arrive((dk_in, dv_in)[which], kout_recv.at[which])
         for slot in range(1, rows):
             target[...] += (dk_in, dv_in)[which][slot].astype(jnp.float32)

time: 28.6 us -> 28.5 us (level)
  no operation moved by 1% of the time
where the time goes in v5:
time: 28.5 us; the launch traced here: 28.3 us
  Pallas kernels  27.6 us (97%)
  between operations  0.64 us (2%)
    pallas_call x1, Pallas kernels, local(): pl.pallas_call(functools.partial(kernel, rows, cols, halves), out_shape=t...  26.9 us
    pallas_call x1, Pallas kernels, local(): pl.pallas_call(functools.partial(hand_on, len(shapes)), out_shape=shapes,...  0.73 us

profile of v5, /device:TPU:0, one launch (start us, length us, event | category | flops | bytes accessed | tf_op | source)
XLA Modules:
  0.0 28.3 jit_solution(11749855153440267157)
XLA Ops:
  0.6 26.9 %shard_map.101 = (bf16[128,128]{1,0:T(8,128)(2,1)S(1)}, f32[128,128]{1,0:T(8,128)S(1)}, f32[128,128]{1,0:T(8,128)S(1)}, f32[128,128]{1,0:T(8,128)S(1)}, f32[128]{0:T(128)S(1)}) custom-call(bf16[128,128]{1,0:T(8,128)(2,1)} %q_hbm.1, bf16[128,128]{1,0:T(8,128)(2,1)} %k_hbm.1, bf16[128,128]{1,0:T(8,128)(2,1)} %v_hbm.1, f32[128]{0:T(128)} %gate_hbm.1, ...), custom_call_target="tpu_custom_call" | custom-call | tf_op jit(solution)/shard_map/pallas_call | solution.py:524
  27.5 0.7 %shard_map.102 = (bf16[128,128]{1,0:T(8,128)(2,1)}, f32[128,128]{1,0:T(8,128)}, f32[128,128]{1,0:T(8,128)}, f32[128,128]{1,0:T(8,128)}, f32[128]{0:T(128)}) custom-call(bf16[128,128]{1,0:T(8,128)(2,1)S(1)} %get-tuple-element.10.refs_0_, f32[128,128]{1,0:T(8,128)S(1)} %get-tuple-element.11.refs_1_, f32[128,128]{1,0:T(8,128)S(1)} %get-tuple-element.12.refs_2_, ...), custom_call_target="tpu_custom_call" | custom-call | tf_op jit(solution)/shard_map/pallas_call | solution.py:576
